TPU v7x, 32 devices: a whole 2x2x4 slice. The times are simulated.
32 devices in a mesh: cd: 8 (over z, y), ab: 4 (over x, core).
Axes of the slice: x: 2, y: 2, z: 4, core: 2. Of those that a mesh axis runs over, the one named last changes fastest.
Arguments:
- amplitudes: bfloat16 [512, 8, 800], P('cd', None, 'ab'), may hold values from -6 to 6
- integrals: bfloat16 [8, 800, 2048], P('cd', None, 'ab'), may hold values from -0.078125 to 0.078125
Outputs:
- ladder: float32 [512, 2048], P('cd', 'ab')
All inputs are finite; a program needn't handle non-finite values.
Results may differ from a plain program's by a relative error of at most 0.0003.
Values may be sent and summed in bfloat16 or wider, within the bound.
A program may use at most 64 MiB of HBM per device.

v0:
```python
import jax
import jax.numpy as jnp
from jax import lax
from jax.sharding import PartitionSpec as P


def on_device(amplitudes, integrals):
    c_local, d_width, ab_local = integrals.shape
    assembled = lax.all_gather(amplitudes, "ab", axis=2, tiled=True)
    complete = lax.all_to_all(assembled, "cd", split_axis=1, concat_axis=0, tiled=True)
    flat = complete.reshape(complete.shape[0], c_local * d_width)
    slab = integrals.reshape(c_local * d_width, ab_local)
    return lax.psum_scatter(
        jnp.dot(flat, slab, preferred_element_type=jnp.float32),
        "cd",
        scatter_dimension=0,
        tiled=True,
    )


def solution(mesh):
    in_specs = (P("cd", None, "ab"), P("cd", None, "ab"))
    out_specs = P("cd", "ab")
    return jax.shard_map(
        on_device, mesh=mesh, in_specs=in_specs, out_specs=out_specs, check_vma=False
    )
```

profile of v0, /device:TPU:0, one launch (start us, length us, event | category | flops | bytes accessed | tf_op | source)
XLA Modules:
  0.0 125.0 jit_solution(4527043416997278588)
XLA Ops:
  6.5 0.0 copy-start
  6.5 0.0 reduce-scatter.2.cloned.1.call-start
  6.5 1.4 %copy.4 = bf16[64,8,200]{0,1,2:T(8,128)(2,1)S(1)} copy(bf16[64,8,200]{2,1,0:T(8,128)(2,1)} %param.2) | data formatting | bytes 409600 | tf_op args[0]
  8.0 14.7 %all_gather.3 = bf16[64,8,800]{0,1,2:T(8,128)(2,1)S(1)} all-gather(bf16[64,8,200]{0,1,2:T(8,128)(2,1)S(1)} %copy.4), channel_id=1, replica_groups=mesh['cd'=8,'ab'=4] {'ab'}, dimensions={2}, use_global_device_ids=true | all-gather | bytes 1024000 | tf_op jit(solution)/shard_map/all_gather | solution.py:9
  22.6 1.9 %copy.5 = bf16[64,8,800]{2,0,1:T(8,128)(2,1)S(1)} copy(bf16[64,8,800]{0,1,2:T(8,128)(2,1)S(1)} %all_gather.3) | data formatting | bytes 1638400 | tf_op jit(solution)/shard_map/all_gather | solution.py:9
  24.6 29.4 %all_to_all.15 = bf16[64,8,800]{2,0,1:T(8,128)(2,1)S(1)} all-to-all(bf16[64,8,800]{2,0,1:T(8,128)(2,1)S(1)} %copy.5), channel_id=1, replica_groups=mesh['cd'=8,'ab'=4] {'cd'}, dimensions={1} | all-to-all | bytes 1638400 | tf_op jit(solution)/shard_map/all_to_all | solution.py:10
  54.0 0.0 copy-done
  54.0 1.7 %fusion = f32[512,512]{1,0:T(8,128)} fusion(bf16[512,800]{1,0:T(8,128)(2,1)S(1)} %bitcast.9, bf16[1,800,512]{2,1,0:T(8,128)(2,1)S(1)} %copy-done), kind=kOutput, calls=%fused_computation | convolution fusion | flops 419430400 | bytes 2686976 | tf_op jit(solution)/shard_map/dot_general | solution.py:14
  55.7 0.0 reduce-scatter.2.cloned.1.call-update
  55.7 62.4 %reduce-scatter.2.cloned.1.call-done = f32[64,512]{1,0:T(8,128)} async-done(((f32[512,512]{1,0:T(8,128)}), f32[64,512]{1,0:T(8,128)}) %reduce-scatter.2.cloned.1.call-update) | async-done | bytes 131088 | tf_op jit(solution)/shard_map/reduce_scatter | solution.py:13
Async XLA Ops:
  6.5 47.5 %copy-start = (bf16[1,800,512]{2,1,0:T(8,128)(2,1)S(1)}, bf16[1,800,512]{2,1,0:T(8,128)(2,1)}, u32[]{:S(2)}) copy-start(bf16[1,800,512]{2,1,0:T(8,128)(2,1)} %param.3) | copy-start | bytes 2457604
  6.5 111.6 %reduce-scatter.2.cloned.1.call-start = ((), (), s32[]{:S(2)}) async-start(), calls=%async_computation.2 | async-start | bytes 1179648 | tf_op jit(solution)/shard_map/reduce_scatter | solution.py:13
Sparse Core Ops, SparseCore 0:
  55.8 62.2 reduce-scatter.1
where the time goes:
time: 125 us
  waiting for transfers between devices  62.4 us (50%)
  blocking collectives  44.1 us (35%)
  between operations  13.4 us (11%)
  local copies, waits for them, and re-layouts  3.34 us (3%)
  matrix products  1.68 us (1%)
    reduce_scatter x1, waiting for transfers between devices, on_device(): lax.psum_scatter(jnp.dot(flat, slab, preferred_element_type=jnp.float32),...  62.4 us
    all_to_all x1, blocking collectives, on_device(): lax.all_to_all(assembled, 'cd', split_axis=1, concat_axis=0, tiled=True)  29.4 us
    all_gather x1, blocking collectives, on_device(): assembled = lax.all_gather(amplitudes, 'ab', axis=2, tiled=True)  14.7 us
  transfers between devices with their start and end apart: 1, of which 1 were waited for; matrix products, arithmetic and copies ran while one was open for 0% of the time, Pallas kernels for 0%

commit v1 on v0

--- a/solution.py
+++ b/solution.py
@@ -1,13 +1,39 @@
+import functools
 import jax
 import jax.numpy as jnp
 from jax import lax
 from jax.sharding import PartitionSpec as P
 
 
+def obtain_rails_on(x_in, which_dim, row_dim):
+    right_arr = lax.axis_size("cd")
+    local_out = lax.axis_index("cd")
+    spare, found_now = (right_arr, local_out)
+    heard = x_in.shape[which_dim] // spare
+    value_now = list(x_in.shape)
+    value_now[which_dim] = heard
+    y = value_now[row_dim]
+    value_now[row_dim] = y * spare
+    piece_now = jnp.zeros(value_now, x_in.dtype)
+    for i in range(spare):
+        local_next = lax.dynamic_slice_in_dim(x_in, (found_now ^ i) * heard, heard, axis=which_dim)
+        if i:
+            local_next = lax.ppermute(
+                local_next, "cd", [(src_i, src_i ^ i) for src_i in range(spare)]
+            )
+        piece_now = lax.dynamic_update_slice_in_dim(
+            piece_now, local_next, (found_now ^ i) * y, axis=row_dim
+        )
+    return piece_now
+
+
+produce_spots = functools.partial(obtain_rails_on, which_dim=1, row_dim=0)
+
+
 def on_device(amplitudes, integrals):
     c_local, d_width, ab_local = integrals.shape
     assembled = lax.all_gather(amplitudes, "ab", axis=2, tiled=True)
-    complete = lax.all_to_all(assembled, "cd", split_axis=1, concat_axis=0, tiled=True)
+    complete = produce_spots(assembled)
     flat = complete.reshape(complete.shape[0], c_local * d_width)
     slab = integrals.reshape(c_local * d_width, ab_local)
     return lax.psum_scatter(

time: 125 us -> 132 us (1.056)
  blocking collectives: 44.1 us -> 14.7 us
  waiting for transfers between devices: 62.4 us -> 75.7 us
  local copies, waits for them, and re-layouts: 3.34 us -> 15 us
  starting transfers between devices: 0.01 us -> 11.4 us
    all_to_all x1 -> x0, blocking collectives: 29.4 us -> none  [on_device(): lax.all_to_all(assembled, 'cd', split_axis=1, concat_axis=0, tiled=True)]
    ppermute x0 -> x7, starting transfers between devices: none -> 11.4 us  [obtain_rails_on(): lax.ppermute(local_next, 'cd', [(src_i, src_i ^ i) for src_i in range(spa...]
    unnamed x3 -> x17, local copies, waits for them, and re-layouts: 1.41 us -> 10.4 us
    ppermute x0 -> x7, waiting for transfers between devices: none -> 8.28 us  [obtain_rails_on(): lax.ppermute(local_next, 'cd', [(src_i, src_i ^ i) for src_i in range(spa...]
    reduce_scatter x1, waiting for transfers between devices: 62.4 us -> 67.4 us  [on_device(): lax.psum_scatter(jnp.dot(flat, slab, preferred_element_type=jnp.float32),...]
    dynamic_slice x0 -> x1, local copies, waits for them, and re-layouts: none -> 4.34 us  [obtain_rails_on(): lax.dynamic_slice_in_dim(x_in, (found_now ^ i) * heard, heard, axis=which...]
    all_gather x1 -> x0, local copies, waits for them, and re-layouts: 1.93 us -> none  [on_device(): assembled = lax.all_gather(amplitudes, 'ab', axis=2, tiled=True)]
  transfers between devices with their start and end apart: 1 -> 8, of which waited for: 1 -> 2; matrix products, arithmetic and copies ran while one was open for 0% -> 6% of each run, Pallas kernels for 0% -> 0%
where the time goes in v1:
time: 132 us
  waiting for transfers between devices  75.7 us (57%)
  local copies, waits for them, and re-layouts  15 us (11%)
  blocking collectives  14.7 us (11%)
  between operations  13.6 us (10%)
  starting transfers between devices  11.4 us (9%)
  matrix products  1.68 us (1%)
    reduce_scatter x1, waiting for transfers between devices, on_device(): lax.psum_scatter(jnp.dot(flat, slab, preferred_element_type=jnp.float32),...  67.4 us
    all_gather x1, blocking collectives, on_device(): assembled = lax.all_gather(amplitudes, 'ab', axis=2, tiled=True)  14.7 us
    ppermute x7, starting transfers between devices, obtain_rails_on(): lax.ppermute(local_next, 'cd', [(src_i, src_i ^ i) for src_i in range(spa...  11.4 us
    unnamed x17, local copies, waits for them, and re-layouts  10.4 us
    ppermute x7, waiting for transfers between devices, obtain_rails_on(): lax.ppermute(local_next, 'cd', [(src_i, src_i ^ i) for src_i in range(spa...  8.28 us
    dynamic_slice x1, local copies, waits for them, and re-layouts, obtain_rails_on(): lax.dynamic_slice_in_dim(x_in, (found_now ^ i) * heard, heard, axis=which...  4.34 us
  transfers between devices with their start and end apart: 8, of which 2 were waited for; matrix products, arithmetic and copies ran while one was open for 6% of the time, Pallas kernels for 0%

profile of v1, /device:TPU:0, one launch (start us, length us, event | category | flops | bytes accessed | tf_op | source)
XLA Modules:
  0.0 132.1 jit_solution(8542994861519288075)
XLA Ops:
  6.5 0.0 copy-start
  6.5 0.0 reduce-scatter.2.cloned.1.call-start
  6.5 1.4 %copy.4 = bf16[64,8,200]{0,1,2:T(8,128)(2,1)S(1)} copy(bf16[64,8,200]{2,1,0:T(8,128)(2,1)} %param.2) | data formatting | bytes 409600 | tf_op args[0]
  8.0 14.7 %all_gather.3 = bf16[64,8,800]{0,1,2:T(8,128)(2,1)S(1)} all-gather(bf16[64,8,200]{0,1,2:T(8,128)(2,1)S(1)} %copy.4), channel_id=1, replica_groups=mesh['cd'=8,'ab'=4] {'ab'}, dimensions={2}, use_global_device_ids=true | all-gather | bytes 1024000 | tf_op jit(solution)/shard_map/all_gather | solution.py:35
  22.6 4.3 %constant_dynamic-slice_fusion = (bf16[64,1,800]{0,1,2:T(2,128)(2,1)S(1)}, bf16[64,1,800]{0,1,2:T(2,128)(2,1)S(1)}, bf16[64,1,800]{0,1,2:T(2,128)(2,1)}, bf16[64...) fusion(bf16[64,8,800]{0,1,2:T(8,128)(2,1)S(1)} %all_gather.3, ...), kind=kLoop, calls=%fused_computation.10 | loop fusion | bytes 1638432 | tf_op jit(solution)/shard_map/dynamic_slice | solution.py:19
  27.0 0.0 copy-start.3
  27.0 0.0 copy-start.2
  27.0 0.0 copy-start.1
  27.0 1.9 %copy.14 = bf16[64,1,800]{2,0,1:T(8,128)(2,1)} copy(bf16[64,1,800]{0,1,2:T(2,128)(2,1)} %get-tuple-element.11) | data formatting | bytes 204800
  28.9 1.5 %collective-permute-start = (bf16[64,1,800]{2,0,1:T(8,128)(2,1)}, bf16[64,1,800]{2,0,1:T(8,128)(2,1)S(1)}, u32[]{:S(2)}, u32[]{:S(2)}) collective-permute-start(bf16[64,1,800]{2,0,1:T(8,128)(2,1)} %copy.14), channel_id=1, source_target_pairs={{0,4},{4,0},{8,12},{12,8},{16,20},{20,16},{24,28},{28,24},{1,5},{5... | collective-permute-start | bytes 307208 | tf_op jit(solution)/shard_map/ppermute | solution.py:21
  30.4 1.8 %copy.15 = bf16[64,1,800]{2,0,1:T(8,128)(2,1)} copy(bf16[64,1,800]{0,1,2:T(2,128)(2,1)} %get-tuple-element.10) | data formatting | bytes 204800
  32.2 1.6 %collective-permute-start.1 = (bf16[64,1,800]{2,0,1:T(8,128)(2,1)}, bf16[64,1,800]{2,0,1:T(8,128)(2,1)S(1)}, u32[]{:S(2)}, u32[]{:S(2)}) collective-permute-start(bf16[64,1,800]{2,0,1:T(8,128)(2,1)} %copy.15), channel_id=1, source_target_pairs={{0,8},{4,12},{8,0},{12,4},{16,24},{20,28},{24,16},{28,20},{1,9},{5... | collective-permute-start | bytes 307208 | tf_op jit(solution)/shard_map/ppermute | solution.py:21
  33.8 1.8 %copy.16 = bf16[64,1,800]{2,0,1:T(8,128)(2,1)} copy(bf16[64,1,800]{0,1,2:T(2,128)(2,1)} %get-tuple-element.9) | data formatting | bytes 204800
  35.6 0.4 collective-permute-start.2
  36.0 0.0 copy-done.3
  36.0 0.6 copy.17
  36.6 2.7 %collective-permute-start.3 = (bf16[64,1,800]{2,0,1:T(8,128)(2,1)S(1)}, bf16[64,1,800]{2,0,1:T(8,128)(2,1)S(1)}, u32[]{:S(2)}, u32[]{:S(2)}) collective-permute-start(bf16[64,1,800]{2,0,1:T(8,128)(2,1)S(1)} %copy.17), channel_id=1, source_target_pairs={{0,16},{4,20},{8,24},{12,28},{16,0},{20,4},{24,8},{28,12},{1,17},{... | collective-permute-start | bytes 307208 | tf_op jit(solution)/shard_map/ppermute | solution.py:21
  39.3 0.0 copy-done.2
  39.3 0.6 copy.18
  39.9 1.4 %collective-permute-start.4 = (bf16[64,1,800]{2,0,1:T(8,128)(2,1)S(1)}, bf16[64,1,800]{2,0,1:T(8,128)(2,1)S(1)}, u32[]{:S(2)}, u32[]{:S(2)}) collective-permute-start(bf16[64,1,800]{2,0,1:T(8,128)(2,1)S(1)} %copy.18), channel_id=1, source_target_pairs={{0,20},{4,16},{8,28},{12,24},{16,4},{20,0},{24,12},{28,8},{1,21},{... | collective-permute-start | bytes 307208 | tf_op jit(solution)/shard_map/ppermute | solution.py:21
  41.2 0.0 copy-done.1
  41.2 0.6 copy.13
  41.8 0.1 reshape.38
  42.0 1.2 copy.19
  43.1 0.6 copy.20
  43.8 0.0 collective-permute-done
  43.8 3.7 %collective-permute-start.5 = (bf16[64,1,800]{2,0,1:T(8,128)(2,1)}, bf16[64,1,800]{2,0,1:T(8,128)(2,1)S(1)}, u32[]{:S(2)}, u32[]{:S(2)}) collective-permute-start(bf16[64,1,800]{2,0,1:T(8,128)(2,1)} %copy.19), channel_id=1, source_target_pairs={{0,24},{4,28},{8,16},{12,20},{16,8},{20,12},{24,0},{28,4},{1,25},{... | collective-permute-start | bytes 307208 | tf_op jit(solution)/shard_map/ppermute | solution.py:21
  47.5 0.0 collective-permute-done.1
  47.5 0.2 collective-permute-start.6
  47.7 0.0 collective-permute-done.2
  47.8 0.0 collective-permute-done.3
  47.8 8.3 %collective-permute-done.4 = bf16[64,1,800]{2,0,1:T(8,128)(2,1)S(1)} collective-permute-done((bf16[64,1,800]{2,0,1:T(8,128)(2,1)S(1)}, bf16[64,1,800]{2,0,1:T(8,128)(2,1)S(1)}, u32[]{:S(2)}, u32[]{:S(2)}) %collective-permute-start.4) | collective-permute-done | bytes 102432 | tf_op jit(solution)/shard_map/ppermute | solution.py:21
  56.1 0.0 collective-permute-done.5
  56.1 0.0 collective-permute-done.6
  56.1 0.0 copy-done
  56.2 1.7 %fusion = f32[512,512]{1,0:T(8,128)} fusion(bf16[512,800]{1,0:T(8,128)(2,1)S(1)} %bitcast_dynamic-update-slice_fusion, bf16[1,800,512]{2,1,0:T(8,128)(2,1)S(1)} %copy-done), kind=kOutput, calls=%fused_computation | convolution fusion | flops 419430400 | bytes 2686976 | tf_op jit(solution)/shard_map/dot_general | solution.py:40
  57.8 0.0 reduce-scatter.2.cloned.1.call-update
  57.9 67.4 %reduce-scatter.2.cloned.1.call-done = f32[64,512]{1,0:T(8,128)} async-done(((f32[512,512]{1,0:T(8,128)}), f32[64,512]{1,0:T(8,128)}) %reduce-scatter.2.cloned.1.call-update) | async-done | bytes 131088 | tf_op jit(solution)/shard_map/reduce_scatter | solution.py:39
  (8 shorter events, 0.2 us)
Async XLA Ops:
  6.5 49.6 %copy-start = (bf16[1,800,512]{2,1,0:T(8,128)(2,1)S(1)}, bf16[1,800,512]{2,1,0:T(8,128)(2,1)}, u32[]{:S(2)}) copy-start(bf16[1,800,512]{2,1,0:T(8,128)(2,1)} %param.3) | copy-start | bytes 2457604
  6.5 118.7 %reduce-scatter.2.cloned.1.call-start = ((), (), s32[]{:S(2)}) async-start(), calls=%async_computation.1 | async-start | bytes 1179648 | tf_op jit(solution)/shard_map/reduce_scatter | solution.py:39
  27.0 9.1 %copy-start.3 = (bf16[64,1,800]{0,1,2:T(2,128)(2,1)S(1)}, bf16[64,1,800]{0,1,2:T(2,128)(2,1)}, u32[]{:S(2)}) copy-start(bf16[64,1,800]{0,1,2:T(2,128)(2,1)} %get-tuple-element.8) | copy-start | bytes 307204
  27.0 12.3 %copy-start.2 = (bf16[64,1,800]{0,1,2:T(2,128)(2,1)S(1)}, bf16[64,1,800]{0,1,2:T(2,128)(2,1)}, u32[]{:S(2)}) copy-start(bf16[64,1,800]{0,1,2:T(2,128)(2,1)} %get-tuple-element.7) | copy-start | bytes 307204
  27.0 14.2 %copy-start.1 = (bf16[64,1,800]{0,1,2:T(2,128)(2,1)S(1)}, bf16[64,1,800]{0,1,2:T(2,128)(2,1)}, u32[]{:S(2)}) copy-start(bf16[64,1,800]{0,1,2:T(2,128)(2,1)} %get-tuple-element.12) | copy-start | bytes 307204
  28.9 14.9 %collective-permute-start = (bf16[64,1,800]{2,0,1:T(8,128)(2,1)}, bf16[64,1,800]{2,0,1:T(8,128)(2,1)S(1)}, u32[]{:S(2)}, u32[]{:S(2)}) collective-permute-start(bf16[64,1,800]{2,0,1:T(8,128)(2,1)} %copy.14), channel_id=1, source_target_pairs={{0,4},{4,0},{8,12},{12,8},{16,20},{20,16},{24,28},{28,24},{1,5},{5... | collective-permute-start | bytes 307208 | tf_op jit(solution)/shard_map/ppermute | solution.py:21
  32.2 15.2 %collective-permute-start.1 = (bf16[64,1,800]{2,0,1:T(8,128)(2,1)}, bf16[64,1,800]{2,0,1:T(8,128)(2,1)S(1)}, u32[]{:S(2)}, u32[]{:S(2)}) collective-permute-start(bf16[64,1,800]{2,0,1:T(8,128)(2,1)} %copy.15), channel_id=1, source_target_pairs={{0,8},{4,12},{8,0},{12,4},{16,24},{20,28},{24,16},{28,20},{1,9},{5... | collective-permute-start | bytes 307208 | tf_op jit(solution)/shard_map/ppermute | solution.py:21
  35.6 12.1 %collective-permute-start.2 = (bf16[64,1,800]{2,0,1:T(8,128)(2,1)}, bf16[64,1,800]{2,0,1:T(8,128)(2,1)S(1)}, u32[]{:S(2)}, u32[]{:S(2)}) collective-permute-start(bf16[64,1,800]{2,0,1:T(8,128)(2,1)} %copy.16), channel_id=1, source_target_pairs={{0,12},{4,8},{8,4},{12,0},{16,28},{20,24},{24,20},{28,16},{1,13},{... | collective-permute-start | bytes 307208 | tf_op jit(solution)/shard_map/ppermute | solution.py:21
  36.6 11.1 %collective-permute-start.3 = (bf16[64,1,800]{2,0,1:T(8,128)(2,1)S(1)}, bf16[64,1,800]{2,0,1:T(8,128)(2,1)S(1)}, u32[]{:S(2)}, u32[]{:S(2)}) collective-permute-start(bf16[64,1,800]{2,0,1:T(8,128)(2,1)S(1)} %copy.17), channel_id=1, source_target_pairs={{0,16},{4,20},{8,24},{12,28},{16,0},{20,4},{24,8},{28,12},{1,17},{... | collective-permute-start | bytes 307208 | tf_op jit(solution)/shard_map/ppermute | solution.py:21
  39.9 16.2 %collective-permute-start.4 = (bf16[64,1,800]{2,0,1:T(8,128)(2,1)S(1)}, bf16[64,1,800]{2,0,1:T(8,128)(2,1)S(1)}, u32[]{:S(2)}, u32[]{:S(2)}) collective-permute-start(bf16[64,1,800]{2,0,1:T(8,128)(2,1)S(1)} %copy.18), channel_id=1, source_target_pairs={{0,20},{4,16},{8,28},{12,24},{16,4},{20,0},{24,12},{28,8},{1,21},{... | collective-permute-start | bytes 307208 | tf_op jit(solution)/shard_map/ppermute | solution.py:21
  43.8 12.3 %collective-permute-start.5 = (bf16[64,1,800]{2,0,1:T(8,128)(2,1)}, bf16[64,1,800]{2,0,1:T(8,128)(2,1)S(1)}, u32[]{:S(2)}, u32[]{:S(2)}) collective-permute-start(bf16[64,1,800]{2,0,1:T(8,128)(2,1)} %copy.19), channel_id=1, source_target_pairs={{0,24},{4,28},{8,16},{12,20},{16,8},{20,12},{24,0},{28,4},{1,25},{... | collective-permute-start | bytes 307208 | tf_op jit(solution)/shard_map/ppermute | solution.py:21
  47.5 8.6 %collective-permute-start.6 = (bf16[64,1,800]{2,0,1:T(8,128)(2,1)S(1)}, bf16[64,1,800]{2,0,1:T(8,128)(2,1)S(1)}, u32[]{:S(2)}, u32[]{:S(2)}) collective-permute-start(bf16[64,1,800]{2,0,1:T(8,128)(2,1)S(1)} %copy.20), channel_id=1, source_target_pairs={{0,28},{4,24},{8,20},{12,16},{16,12},{20,8},{24,4},{28,0},{1,29},{... | collective-permute-start | bytes 307208 | tf_op jit(solution)/shard_map/ppermute | solution.py:21
Sparse Core Ops, SparseCore 0:
  58.0 67.2 reduce-scatter.1
